TPU v7x, 32 devices: a whole 2x2x4 slice. The times are simulated.
32 devices in a mesh: groups: 2 (over y), fsdp: 4 (over z), dp: 2 (over x), sub: 2 (over core).
Axes of the slice: x: 2, y: 2, z: 4, core: 2. Of those that a mesh axis runs over, the one named last changes fastest.
Arguments:
- hidden: bfloat16 [32, 64, 28672], P(('groups', 'fsdp', 'dp'), None, 'sub'), parts along dimension 0, may hold values from -6 to 6
- out_grad: bfloat16 [32, 64, 8192], P(('groups', 'fsdp', 'dp'), None, 'sub'), parts along dimension 0, may hold values from -6 to 6
- proj_in: bfloat16 [2, 14336, 64], P('sub', 'fsdp'), may hold values from -0.03125 to 0.03125
- proj_out: bfloat16 [2, 4096, 64], P('sub', 'fsdp'), may hold values from -0.0625 to 0.0625
- queries: bfloat16 [1024, 4096], P('fsdp', 'sub'), may hold values from -6 to 6
- lengths: int32 [32], P(('groups', 'fsdp', 'dp')), parts along dimension 0, may hold values from 1 to 64, 768 in all
Outputs:
- covariance: float32 [8192, 4096], P(('groups', 'fsdp'), ('dp', 'sub')), parts along dimension 0
- scores: float32 [32, 1024], P(('groups', 'fsdp', 'dp')), parts along dimension 0
There are 2 independent parts, one for each index of `groups`. A program takes and returns all parts, laid end to end along the dimension named above; an argument that names none is the same for every part. Nothing has to cross between parts.
Inputs may be any that keep to these rules, and one draw needn't show every extreme that they name: lengths[e] is the number of live token slots of example e; slots from lengths[e] on are padding; in each part along groups the lengths sum to 768, and some example of each part fills all 64 slots.
All inputs are finite; a program needn't handle non-finite values.
Results may differ from a plain program's by a relative error of at most 0.0041.
Values may be sent and summed in bfloat16 or wider, within the bound.
A program may use at most 128 MiB of HBM per device.

v0:
```python
import math

import jax
import jax.numpy as jnp
from jax import lax
from jax.sharding import PartitionSpec as P


def body(hidden, out_grad, proj_in, proj_out, queries, lengths):
    examples, slot_len, half_hidden = hidden.shape
    half_model = out_grad.shape[2]
    factor_width = proj_in.shape[2]
    tok_rows = examples * slot_len
    rows_in = hidden.reshape(tok_rows, half_hidden)
    rows_out = out_grad.reshape(tok_rows, half_model)
    columns = rows_in
    inputs_part = jnp.dot(
        columns,
        lax.all_gather(proj_in, "fsdp", axis=1, tiled=True)[0],
        preferred_element_type=jnp.float32,
    )
    columns = rows_out
    grads_part = jnp.dot(
        columns,
        lax.all_gather(proj_out, "fsdp", axis=1, tiled=True)[0],
        preferred_element_type=jnp.float32,
    )
    partial_value = jnp.concatenate((grads_part, inputs_part), axis=1)
    summed = lax.psum(partial_value, "sub")
    low_grads = summed[:, :factor_width].reshape(examples, slot_len, factor_width)
    low_inputs = summed[:, factor_width:].reshape(examples, slot_len, factor_width)
    live_mask = (jnp.arange(slot_len, dtype=jnp.int32)[None, :] < lengths[:, None]).astype(
        jnp.float32
    )
    low_grads = low_grads * live_mask[:, :, None]
    encoded = jnp.einsum(
        "eta,etb->eab", low_grads, low_inputs, precision=lax.Precision.HIGHEST
    ) / math.sqrt(slot_len)
    encoded_dim = factor_width * factor_width
    encoded = encoded.reshape(examples, encoded_dim).astype(jnp.bfloat16)
    fsdp_size = lax.axis_size("fsdp")
    dp_size = lax.axis_size("dp")
    sub_size = lax.axis_size("sub")
    row_block = encoded_dim // fsdp_size
    col_block = encoded_dim // (dp_size * sub_size)
    col_half = encoded_dim // sub_size
    gathered = lax.all_gather(encoded, "fsdp", axis=0, tiled=True)
    strided = gathered.reshape(gathered.shape[0], dp_size, sub_size, col_block)
    right_cols = lax.dynamic_index_in_dim(strided, lax.axis_index("sub"), 2, keepdims=False)
    right_cols = right_cols.reshape(gathered.shape[0], dp_size * col_block)
    partial_cov = lax.dot_general(
        lax.dynamic_slice_in_dim(gathered, lax.axis_index("fsdp") * row_block, row_block, 1),
        right_cols,
        (((0,), (0,)), ((), ())),
        preferred_element_type=jnp.float32,
    )
    covariance = lax.psum_scatter(partial_cov, "dp", scatter_dimension=1, tiled=True) / (
        gathered.shape[0] * dp_size
    )
    own_half = lax.dynamic_slice_in_dim(encoded, lax.axis_index("sub") * col_half, col_half, 1)
    partial_scores = lax.dot_general(
        own_half,
        lax.all_gather(queries, "fsdp", axis=0, tiled=True),
        (((1,), (1,)), ((), ())),
        preferred_element_type=jnp.float32,
    )
    scores = lax.psum(partial_scores, "sub") / math.sqrt(encoded_dim)
    return (covariance, scores)


def solution(mesh):
    placed = (
        P(("groups", "fsdp", "dp"), None, "sub"),
        P(("groups", "fsdp", "dp"), None, "sub"),
        P("sub", "fsdp", None),
        P("sub", "fsdp", None),
        P("fsdp", "sub"),
        P(("groups", "fsdp", "dp")),
    )
    return jax.shard_map(
        body,
        mesh=mesh,
        in_specs=placed,
        out_specs=(P(("groups", "fsdp"), ("dp", "sub")), P(("groups", "fsdp", "dp"), None)),
        check_vma=False,
    )
```

profile of v0, /device:TPU:0, one launch (start us, length us, event | category | flops | bytes accessed | tf_op | source)
XLA Modules:
  0.0 271.8 jit_solution(2435906160909390401)
XLA Ops:
  7.2 0.0 copy-start
  7.2 0.0 all-gather.4.cloned.1.call-start
  7.2 0.7 all-gather.4.cloned.1.call-update
  7.9 0.0 all-reduce.2.cloned.1.call-start
  8.0 19.3 %all_gather.12 = bf16[1,4096,64]{1,2,0:T(8,128)(2,1)S(1)} all-gather(bf16[1,1024,64]{1,2,0:T(8,128)(2,1)} %param.9), channel_id=1, replica_groups=mesh['groups'=2,'fsdp'=4,'dp'=2,'sub'=2] {'fsdp'}, dimensions={1}, use_global_device_ids=true | all-gather | bytes 655360 | tf_op jit(solution)/shard_map/all_gather | solution.py:25
  27.3 0.5 fusion.3
  27.8 27.8 %all-gather.4.cloned.1.call-done = bf16[1,14336,64]{1,2,0:T(8,128)(2,1)} async-done(((bf16[1,3584,64]{1,2,0:T(8,128)(2,1)}), bf16[1,14336,64]{1,2,0:T(8,128)(2,1)}) %all-gather.4.cloned.1.call-update) | async-done | bytes 1835024 | tf_op jit(solution)/shard_map/all_gather | solution.py:19
  55.6 4.0 %fusion = f32[128,64]{0,1:T(8,128)S(1)} fusion(bf16[128,14336]{1,0:T(8,128)(2,1)} %bitcast.19, bf16[1,14336,64]{1,2,0:T(8,128)(2,1)} %all-gather.4.cloned.1.call-done), kind=kOutput, calls=%fused_computation.1 | convolution fusion | flops 234881024 | bytes 5537792 | tf_op jit(solution)/shard_map/dot_general | solution.py:17
  59.6 0.6 pad_maximum_fusion
  60.2 0.0 all-reduce.2.cloned.1.call-update
  60.3 0.0 all-gather.6.cloned.1.call-start
  60.3 0.7 all-gather.6.cloned.1.call-update
  61.0 0.0 reduce-scatter.2.cloned.1.call-start
  61.1 0.1 compare_convert_fusion
  61.1 15.6 %all-reduce.2.cloned.1.call-done = f32[128,128]{0,1:T(8,128)} async-done(((f32[128,128]{0,1:T(8,128)}), f32[128,128]{0,1:T(8,128)}) %all-reduce.2.cloned.1.call-update) | async-done | bytes 65552 | tf_op jit(solution)/shard_map/psum | solution.py:29
  76.8 0.8 fusion.12
  77.5 0.1 reshape.49
  77.6 0.1 copy.16
  77.7 0.2 fusion.2
  77.9 0.1 reshape.53
  78.0 13.5 %all-gather = bf16[4,2,4096]{2,1,0:T(2,128)(2,1)S(1)} all-gather(bf16[1,2,4096]{2,1,0:T(2,128)(2,1)S(1)} %reshape.53), channel_id=1, replica_groups=mesh['groups'=2,'fsdp'=4,'dp'=2,'sub'=2] {'fsdp'}, dimensions={0}, use_global_device_ids=true | all-gather | bytes 81920 | tf_op jit(solution)/shard_map/all_gather | solution.py:47
  91.6 0.1 reshape.51
  91.7 0.2 dynamic-slice_reduce_fusion
  91.9 4.5 %fusion.6 = f32[1024,2048]{1,0:T(8,128)} fusion(bf16[8,2048]{1,0:T(8,128)(2,1)S(1)} %bitcast.21, bf16[8,4096]{1,0:T(8,128)(2,1)S(1)} %reshape.54, s32[]{:T(128)S(6)} %select_n.10), kind=kOutput, calls=%fused_computation.11 | convolution fusion | flops 33554432 | bytes 8437764 | tf_op jit(solution)/shard_map/dot_general | solution.py:51
  96.4 0.0 reduce-scatter.2.cloned.1.call-update
  96.4 0.1 convert_element_type.15
  96.5 63.8 %all-gather.6.cloned.1.call-done = bf16[1024,2048]{1,0:T(8,128)(2,1)} async-done(((bf16[256,2048]{1,0:T(8,128)(2,1)}), bf16[1024,2048]{1,0:T(8,128)(2,1)}) %all-gather.6.cloned.1.call-update) | async-done | bytes 4194320 | tf_op jit(solution)/shard_map/all_gather | solution.py:63
  160.3 3.4 %fusion.8 = f32[2,1024]{1,0:T(2,128)S(1)} fusion(bf16[1024,2048]{1,0:T(8,128)(2,1)} %all-gather.6.cloned.1.call-done, bf16[2,4096]{1,0:T(2,128)(2,1)S(1)} %convert_element_type.15, s32[]{:T(128)S(6)} %select_n.12), kind=kOutput, calls=%fused_computation.13 | convolution fusion | flops 8388608 | bytes 4210692 | tf_op jit(solution)/shard_map/dot_general | solution.py:61
  163.7 2.5 psum.15
  166.2 0.6 broadcast_multiply_fusion.1
  166.8 93.5 %reduce-scatter.2.cloned.1.call-done = f32[1024,1024]{1,0:T(8,128)} async-done(((f32[1024,2048]{1,0:T(8,128)}), f32[1024,1024]{1,0:T(8,128)}) %reduce-scatter.2.cloned.1.call-update) | async-done | bytes 4194320 | tf_op jit(solution)/shard_map/reduce_scatter | solution.py:57
  260.2 5.0 %broadcast_multiply_fusion = f32[1024,1024]{1,0:T(8,128)} fusion(f32[1024,1024]{1,0:T(8,128)} %reduce-scatter.2.cloned.1.call-done), kind=kLoop, calls=%fused_computation | loop fusion | flops 1048576 | bytes 8388608 | tf_op jit(solution)/shard_map/div | solution.py:57
  (5 shorter events, 0.0 us)
Async XLA Ops:
  7.2 20.1 %copy-start = (bf16[2,64,4096]{2,1,0:T(8,128)(2,1)S(1)}, bf16[2,64,4096]{2,1,0:T(8,128)(2,1)}, u32[]{:S(2)}) copy-start(bf16[2,64,4096]{2,1,0:T(8,128)(2,1)} %param.7) | copy-start | bytes 3145732
  7.2 48.4 %all-gather.4.cloned.1.call-start = ((), (), s32[]{:S(2)}) async-start(), calls=%async_computation.1 | async-start | bytes 2293760 | tf_op jit(solution)/shard_map/all_gather | solution.py:19
  7.9 68.8 %all-reduce.2.cloned.1.call-start = ((), (), s32[]{:S(2)}) async-start(), calls=%async_computation.2 | async-start | bytes 131072 | tf_op jit(solution)/shard_map/psum | solution.py:29
  27.3 33.8 %copy-start.1 = (s32[2]{0:T(128)S(1)}, s32[2]{0:T(128)}, u32[]{:S(2)}) copy-start(s32[2]{0:T(128)} %param.11) | copy-start | bytes 28
  60.3 100.0 %all-gather.6.cloned.1.call-start = ((), (), s32[]{:S(2)}) async-start(), calls=%async_computation.4 | async-start | bytes 5242880 | tf_op jit(solution)/shard_map/all_gather | solution.py:63
  61.0 199.2 %reduce-scatter.2.cloned.1.call-start = ((), (), s32[]{:S(2)}) async-start(), calls=%async_computation.3 | async-start | bytes 12582912 | tf_op jit(solution)/shard_map/reduce_scatter | solution.py:57
Sparse Core Ops, SparseCore 0:
  9.6 45.9 all-gather.3
  60.4 16.3 all-reduce.1
  78.3 81.9 all-gather.5
  162.5 97.7 reduce-scatter.1
where the time goes:
time: 272 us
  waiting for transfers between devices  202 us (74%)
  blocking collectives  35.3 us (13%)
  between operations  13.8 us (5%)
  matrix products  12.6 us (5%)
  other arithmetic  6.35 us (2%)
    reduce_scatter x1, waiting for transfers between devices, body(): lax.psum_scatter(partial_cov, 'dp', scatter_dimension=1, tiled=True)  93.5 us
    all_gather x1, waiting for transfers between devices, body(): lax.all_gather(queries, 'fsdp', axis=0, tiled=True)  63.8 us
    all_gather x1, waiting for transfers between devices, body(): lax.all_gather(proj_in, 'fsdp', axis=1, tiled=True)[0]  27.8 us
    all_gather x1, blocking collectives, body(): lax.all_gather(proj_out, 'fsdp', axis=1, tiled=True)[0]  19.3 us
    psum x1, waiting for transfers between devices, body(): summed = lax.psum(partial_value, 'sub')  15.6 us
    all_gather x1, blocking collectives, body(): gathered = lax.all_gather(encoded, 'fsdp', axis=0, tiled=True)  13.5 us
  transfers between devices with their start and end apart: 4, of which 4 were waited for; matrix products, arithmetic and copies ran while one was open for 4% of the time, Pallas kernels for 0%

commit v1 on v0

v1 whole, which is shorter than its diff:
```python
import functools
import math

import jax
import jax.numpy as jnp
from jax import lax
from jax.experimental import pallas as pl
from jax.experimental.pallas import tpu as pltpu
from jax.sharding import PartitionSpec as P

MESH = pl.DeviceIdType.MESH
NT = (((1,), (1,)), ((), ()))


def kernel(F, hidden, out_grad, pin, pout, queries, lengths,
           rows_out, cols_out, scores_out,
           buf, hid, ogr, qry, acc, part, summed, gath, flat, enc, spart, sgot,
           local_sem, zs, xs, ys, dxs, dys, zr, xr, yr, dxr, dyr,
           sub_sem, es, er, ss, sr):
    g, f, d, s = (lax.axis_index(n) for n in ("groups", "fsdp", "dp", "sub"))
    W = pin.shape[0]
    kin, kout = pin.shape[1], pout.shape[1]
    L = kin + kout
    half = L // 2
    piece_rows = W // 4
    tokens = hidden.shape[0]
    E = enc.shape[0]

    loads = [
        pltpu.make_async_copy(pin, buf.at[f, :, pl.ds(0, kin)], local_sem.at[0]),
        pltpu.make_async_copy(pout, buf.at[f, :, pl.ds(kin, kout)], local_sem.at[1]),
    ]
    loads += [
        pltpu.make_async_copy(hidden.at[:, pl.ds(k * kin, kin)], hid.at[k], local_sem.at[3 + k])
        for k in range(F)
    ]
    loads += [
        pltpu.make_async_copy(out_grad.at[:, pl.ds(k * kout, kout)], ogr.at[k], local_sem.at[3 + F + k])
        for k in range(F)
    ]
    query_load = pltpu.make_async_copy(queries, qry, local_sem.at[2])
    for load in loads:
        load.start()
    query_load.start()

    barrier = pltpu.get_barrier_semaphore()
    others = [(df, dd, ds) for df in range(F) for dd in range(2) for ds in range(2)][1:]
    for df, dd, ds in others:
        pl.semaphore_signal(
            barrier, inc=1,
            device_id=(g, lax.rem(f + df, F), lax.rem(d + dd, 2), lax.rem(s + ds, 2)),
            device_id_type=MESH,
        )
    pl.semaphore_signal(barrier, inc=1, device_id=(1 - g, f, d, s), device_id_type=MESH)
    pl.semaphore_wait(barrier, len(others) + 1)

    mine = g * 2 + d
    col_x, col_y, col_d = g * 2 + (1 - d), (1 - g) * 2 + d, (1 - g) * 2 + (1 - d)
    dev_x, dev_y = (g, f, 1 - d, s), (1 - g, f, d, s)

    def piece(shard, col, lanes=None):
        rows = pl.ds(pl.multiple_of(col * piece_rows, piece_rows), piece_rows)
        if lanes is None:
            return buf.at[shard, rows, :]
        return buf.at[shard, rows, pl.ds(lanes * half, half)]

    def copy(ref, send, recv, dev):
        return pltpu.make_async_remote_copy(
            src_ref=ref, dst_ref=ref, send_sem=send, recv_sem=recv,
            device_id=dev, device_id_type=MESH,
        )

    def along_z(shard, up):
        dev = (g, f + 1, d, s) if up else (g, f - 1, d, s)
        return copy(piece(shard, mine), zs.at[1 if up else 0, shard], zr.at[shard], dev)

    def to_x(shard):
        return copy(piece(shard, mine), xs.at[shard], xr.at[shard], dev_x)

    def to_y(shard):
        return copy(piece(shard, mine), ys.at[shard], yr.at[shard], dev_y)

    def from_x(shard):
        return copy(piece(shard, col_x), xs.at[shard], xr.at[shard], dev_x)

    def from_y(shard):
        return copy(piece(shard, col_y), ys.at[shard], yr.at[shard], dev_y)

    def x_on_to_y(shard):
        return copy(piece(shard, col_x, 0), dys.at[shard], dyr.at[shard], dev_y)

    def y_on_to_x(shard):
        return copy(piece(shard, col_y, 1), dxs.at[shard], dxr.at[shard], dev_x)

    def diag_by_y(shard):
        return copy(piece(shard, col_d, 0), dys.at[shard], dyr.at[shard], dev_y)

    def diag_by_x(shard):
        return copy(piece(shard, col_d, 1), dxs.at[shard], dxr.at[shard], dev_x)

    def project(shard):
        acc[W:, :] += lax.dot_general(
            buf[shard, :, :kin], hid[shard], NT, preferred_element_type=jnp.float32)
        acc[:W, :] += lax.dot_general(
            buf[shard, :, kin:], ogr[shard], NT, preferred_element_type=jnp.float32)

    def each(t, fn):
        @pl.when(f - t >= 0)
        def _():
            fn(f - t, True)

        @pl.when(f + t < F)
        def _():
            fn(f + t, False)

    loads[0].wait()
    loads[1].wait()

    @pl.when(f > 0)
    def _():
        along_z(f, False).start()

    @pl.when(f < F - 1)
    def _():
        along_z(f, True).start()

    for load in loads[2:]:
        load.wait()
    acc[...] = jnp.zeros_like(acc)
    project(f)

    def arrive(shard, up):
        along_z(shard, up).wait_recv()
        if up:
            @pl.when(f < F - 1)
            def _():
                along_z(shard, True).start()
        else:
            @pl.when(f > 0)
            def _():
                along_z(shard, False).start()
        to_x(shard).start()
        to_y(shard).start()

    def relay(shard, up):
        from_x(shard).wait_recv()
        x_on_to_y(shard).start()
        from_y(shard).wait_recv()
        y_on_to_x(shard).start()

    def finish(shard, up):
        diag_by_y(shard).wait_recv()
        diag_by_x(shard).wait_recv()
        project(shard)

    for t in range(1, F + 2):
        if t < F:
            each(t, arrive)
        if 1 <= t - 1 < F:
            each(t - 1, relay)
        if 1 <= t - 2 < F:
            each(t - 2, finish)

    p_copy = pltpu.make_async_remote_copy(
        src_ref=acc, dst_ref=part, send_sem=sub_sem.at[0], recv_sem=sub_sem.at[1],
        device_id=(g, f, d, 1 - s), device_id_type=MESH,
    )
    p_copy.start()
    p_copy.wait_recv()
    summed[...] = acc[...] + part[...]

    slot = tokens // 2
    lane = lax.broadcasted_iota(jnp.int32, (W // 2, tokens), 1)
    even = summed[pl.ds(0, W // 2, stride=2), :]
    odd = summed[pl.ds(1, W // 2, stride=2), :]
    first = lane < lengths[0]
    second = jnp.logical_and(lane >= slot, lane < slot + lengths[1])
    left = jnp.concatenate(
        [jnp.where(first, even, 0.0), jnp.where(first, odd, 0.0),
         jnp.where(second, even, 0.0), jnp.where(second, odd, 0.0)], axis=0)
    outer = lax.dot_general(
        left, summed[W:, :], NT, precision=lax.Precision.HIGHEST,
        preferred_element_type=jnp.float32) / math.sqrt(slot)
    hw = W // 2
    pair = f * 2 + d
    own = pl.ds(pair * 2, 2)
    for i in range(2):
        both = jnp.concatenate(
            [outer[2 * i * hw:(2 * i + 1) * hw], outer[(2 * i + 1) * hw:(2 * i + 2) * hw]], axis=1)
        gath[pair * 2 + i] = both.astype(jnp.bfloat16)

    shifts = [(df, dd) for df in range(F) for dd in range(2)][1:]

    def enc_copy(k, owner, dev):
        ref = gath.at[pl.ds(owner * 2, 2)]
        return pltpu.make_async_remote_copy(
            src_ref=ref, dst_ref=ref, send_sem=es.at[k], recv_sem=er.at[owner],
            device_id=dev, device_id_type=MESH)

    def peer(df, dd):
        return lax.rem(f + df, F), lax.rem(d + dd, 2)

    for k, (df, dd) in enumerate(shifts):
        pf, pd = peer(df, dd)
        enc_copy(k, pair, (g, pf, pd, s)).start()
    query_load.wait()
    for k, (df, dd) in enumerate(shifts):
        pf, pd = peer(df, dd)
        enc_copy(k, pf * 2 + pd, (g, pf, pd, s)).wait_recv()

    for e in range(E):
        flat[e * hw:(e + 1) * hw, :] = gath[e].astype(jnp.float32)
    for r in range(hw):
        enc[:, r * 128:(r + 1) * 128] = flat[pl.ds(r, E, stride=hw), :].astype(jnp.bfloat16)

    dims = qry.shape[1]
    score = lax.dot_general(
        enc[:, pl.ds(pl.multiple_of(s * dims, dims), dims)], qry[...], NT,
        preferred_element_type=jnp.float32)
    for p in range(E // 2):
        spart[p] = score[2 * p:2 * p + 2, :]
    targets = [(df, ds) for df in range(F) for ds in range(2)]

    def score_copy(k, src, slot_id, dev):
        return pltpu.make_async_remote_copy(
            src_ref=spart.at[src], dst_ref=sgot.at[slot_id],
            send_sem=ss.at[k], recv_sem=sr.at[slot_id],
            device_id=dev, device_id_type=MESH)

    for k, (df, ds) in enumerate(targets[1:]):
        pf, ps = lax.rem(f + df, F), lax.rem(s + ds, 2)
        score_copy(k, pf * 2 + d, f * 2 + s, (g, pf, d, ps)).start()
    sgot[f * 2 + s] = spart[pair]
    nrow, ncol = rows_out.shape[1], cols_out.shape[1]
    rows_out[...] = enc[:, pl.ds(pl.multiple_of(f * nrow, nrow), nrow)]
    cols_out[...] = enc[:, pl.ds(pl.multiple_of((d * 2 + s) * ncol, ncol), ncol)]
    for k, (df, ds) in enumerate(targets[1:]):
        pf, ps = lax.rem(f + df, F), lax.rem(s + ds, 2)
        score_copy(k, pf * 2 + d, pf * 2 + ps, (g, pf, d, ps)).wait_recv()
    nq = qry.shape[0]
    for k in range(F):
        scores_out[:, k * nq:(k + 1) * nq] = (sgot[2 * k] + sgot[2 * k + 1]) / math.sqrt(2 * dims)

    for k, (df, ds) in enumerate(targets[1:]):
        pf, ps = lax.rem(f + df, F), lax.rem(s + ds, 2)
        score_copy(k, pf * 2 + d, f * 2 + s, (g, pf, d, ps)).wait_send()
    for k, (df, dd) in enumerate(shifts):
        pf, pd = peer(df, dd)
        enc_copy(k, pair, (g, pf, pd, s)).wait_send()
    p_copy.wait_send()

    @pl.when(f > 0)
    def _():
        along_z(f, False).wait_send()

    @pl.when(f < F - 1)
    def _():
        along_z(f, True).wait_send()

    def sent(shard, up):
        if up:
            @pl.when(f < F - 1)
            def _():
                along_z(shard, True).wait_send()
        else:
            @pl.when(f > 0)
            def _():
                along_z(shard, False).wait_send()
        to_x(shard).wait_send()
        to_y(shard).wait_send()
        x_on_to_y(shard).wait_send()
        y_on_to_x(shard).wait_send()

    for t in range(1, F):
        each(t, sent)


def fused(F, hidden, out_grad, proj_in, proj_out, queries, lengths):
    examples, slot_len, half_hidden = hidden.shape
    half_model = out_grad.shape[2]
    W = proj_in.shape[2]
    kin, kout = proj_in.shape[1], proj_out.shape[1]
    tokens = examples * slot_len
    nq, dims = queries.shape
    E = F * 2 * examples
    KK = W * W
    any_spec = pl.BlockSpec(memory_space=pl.ANY)
    vmem = pl.BlockSpec(memory_space=pltpu.VMEM)
    bf, f32 = jnp.bfloat16, jnp.float32
    dma = pltpu.SemaphoreType.DMA
    rows, cols, scores = pl.pallas_call(
        functools.partial(kernel, F),
        out_shape=(
            jax.ShapeDtypeStruct((E, KK // F), bf),
            jax.ShapeDtypeStruct((E, KK // 4), bf),
            jax.ShapeDtypeStruct((examples, nq * F), f32),
        ),
        in_specs=[any_spec] * 5 + [pl.BlockSpec(memory_space=pltpu.SMEM)],
        out_specs=(vmem, vmem, vmem),
        scratch_shapes=[
            pltpu.VMEM((F, W, kin + kout), bf),
            pltpu.VMEM((F, tokens, kin), bf),
            pltpu.VMEM((F, tokens, kout), bf),
            pltpu.VMEM((nq, dims), bf),
            pltpu.VMEM((2 * W, tokens), f32),
            pltpu.VMEM((2 * W, tokens), f32),
            pltpu.VMEM((2 * W, tokens), f32),
            pltpu.VMEM((E, W // 2, 2 * W), bf),
            pltpu.VMEM((E * W // 2, 2 * W), f32),
            pltpu.VMEM((E, KK), bf),
            pltpu.VMEM((E // 2, 2, nq), f32),
            pltpu.VMEM((2 * F, 2, nq), f32),
            dma((3 + 2 * F,)),
            dma((2, F)), dma((F,)), dma((F,)), dma((F,)), dma((F,)),
            dma((F,)), dma((F,)), dma((F,)), dma((F,)), dma((F,)),
            dma((2,)),
            dma((2 * F,)), dma((2 * F,)), dma((2 * F,)), dma((2 * F,)),
        ],
        compiler_params=pltpu.CompilerParams(
            collective_id=0, has_side_effects=True, vmem_limit_bytes=60 << 20),
    )(
        hidden.reshape(tokens, half_hidden),
        out_grad.reshape(tokens, half_model),
        jnp.swapaxes(proj_in[0], 0, 1),
        jnp.swapaxes(proj_out[0], 0, 1),
        queries,
        lengths,
    )
    covariance = lax.dot_general(
        rows, cols, (((0,), (0,)), ((), ())), preferred_element_type=f32) / E
    return covariance, scores


def general(hidden, out_grad, proj_in, proj_out, queries, lengths):
    examples, slot_len, half_hidden = hidden.shape
    half_model = out_grad.shape[2]
    W = proj_in.shape[2]
    tokens = examples * slot_len
    f32 = jnp.float32
    inputs_part = jnp.dot(
        hidden.reshape(tokens, half_hidden),
        lax.all_gather(proj_in, "fsdp", axis=1, tiled=True)[0],
        preferred_element_type=f32)
    grads_part = jnp.dot(
        out_grad.reshape(tokens, half_model),
        lax.all_gather(proj_out, "fsdp", axis=1, tiled=True)[0],
        preferred_element_type=f32)
    summed = lax.psum(jnp.concatenate((grads_part, inputs_part), axis=1), "sub")
    low_grads = summed[:, :W].reshape(examples, slot_len, W)
    low_inputs = summed[:, W:].reshape(examples, slot_len, W)
    live = (jnp.arange(slot_len, dtype=jnp.int32)[None, :] < lengths[:, None]).astype(f32)
    encoded = jnp.einsum(
        "eta,etb->eab", low_grads * live[:, :, None], low_inputs,
        precision=lax.Precision.HIGHEST) / math.sqrt(slot_len)
    KK = W * W
    encoded = encoded.reshape(examples, KK).astype(jnp.bfloat16)
    F, Dp, S = lax.axis_size("fsdp"), lax.axis_size("dp"), lax.axis_size("sub")
    everyone = lax.all_gather(encoded, ("fsdp", "dp"), axis=0, tiled=True)
    nrow, ncol, half = KK // F, KK // (Dp * S), KK // S
    rows = lax.dynamic_slice_in_dim(everyone, lax.axis_index("fsdp") * nrow, nrow, 1)
    cols = lax.dynamic_slice_in_dim(
        everyone, (lax.axis_index("dp") * S + lax.axis_index("sub")) * ncol, ncol, 1)
    covariance = lax.dot_general(
        rows, cols, (((0,), (0,)), ((), ())), preferred_element_type=f32) / everyone.shape[0]
    own_half = lax.dynamic_slice_in_dim(encoded, lax.axis_index("sub") * half, half, 1)
    partial_scores = lax.dot_general(
        own_half, lax.all_gather(queries, "fsdp", axis=0, tiled=True),
        (((1,), (1,)), ((), ())), preferred_element_type=f32)
    scores = lax.psum(partial_scores, "sub") / math.sqrt(KK)
    return covariance, scores


def solution(mesh):
    sizes = dict(mesh.shape)
    placed = (
        P(("groups", "fsdp", "dp"), None, "sub"),
        P(("groups", "fsdp", "dp"), None, "sub"),
        P("sub", "fsdp", None),
        P("sub", "fsdp", None),
        P("fsdp", "sub"),
        P(("groups", "fsdp", "dp")),
    )
    square = sizes["groups"] == 2 and sizes["dp"] == 2 and sizes["fsdp"] <= 4
    body = functools.partial(fused, sizes["fsdp"]) if square else general
    return jax.shard_map(
        body,
        mesh=mesh,
        in_specs=placed,
        out_specs=(P(("groups", "fsdp"), ("dp", "sub")), P(("groups", "fsdp", "dp"), None)),
        check_vma=False,
    )
```

time: 272 us -> 47.6 us (0.18)
  waiting for transfers between devices: 202 us -> 0 us
  Pallas kernels: 0 us -> 42.6 us
  blocking collectives: 35.3 us -> 0 us
  between operations: 13.8 us -> 0.65 us
  matrix products: 12.6 us -> 3.53 us
  other arithmetic: 6.35 us -> 0 us
    reduce_scatter x1 -> x0, waiting for transfers between devices: 93.5 us -> none  [body(): lax.psum_scatter(partial_cov, 'dp', scatter_dimension=1, tiled=True)]
    all_gather x2 -> x0, waiting for transfers between devices: 91.6 us -> none  [the longest x1 63.8 us: body(): lax.all_gather(queries, 'fsdp', axis=0, tiled=True)]
    pallas_call x0 -> x1, Pallas kernels: none -> 42.6 us  [fused(): pl.pallas_call(functools.partial(kernel, F), out_shape=(jax.ShapeDtypeStr...]
    all_gather x2 -> x0, blocking collectives: 32.8 us -> none  [the longest x1 19.3 us: body(): lax.all_gather(proj_out, 'fsdp', axis=1, tiled=True)[0]]
    psum x1 -> x0, waiting for transfers between devices: 15.6 us -> none  [body(): summed = lax.psum(partial_value, 'sub')]
    dot_general x5 -> x1, matrix products: 12.6 us -> 3.53 us  [fused(): lax.dot_general(rows, cols, (((0,), (0,)), ((), ())), preferred_element_t...]
    div x2 -> x0, other arithmetic: 5.65 us -> none  [the longest x1 5.04 us: body(): lax.psum_scatter(partial_cov, 'dp', scatter_dimension=1, tiled=True)]
  transfers between devices with their start and end apart: 4 -> 0, of which waited for: 4 -> 0; matrix products, arithmetic and copies ran while one was open for 4% -> 0% of each run, Pallas kernels for 0% -> 0%
where the time goes in v1:
time: 47.6 us; the launch traced here: 47.4 us
  Pallas kernels  42.6 us (89%)
  matrix products  3.53 us (7%)
  between operations  0.65 us (1%)
  local copies, waits for them, and re-layouts  0.6 us (1%)
    pallas_call x1, Pallas kernels, fused(): pl.pallas_call(functools.partial(kernel, F), out_shape=(jax.ShapeDtypeStr...  42.6 us
    dot_general x1, matrix products, fused(): lax.dot_general(rows, cols, (((0,), (0,)), ((), ())), preferred_element_t...  3.53 us

profile of v1, /device:TPU:0, one launch (start us, length us, event | category | flops | bytes accessed | tf_op | source)
XLA Modules:
  0.0 47.4 jit_solution(17420150735814174383)
XLA Ops:
  0.6 42.6 %shard_map.77 = (bf16[16,1024]{1,0:T(8,128)(2,1)}, bf16[16,1024]{1,0:T(8,128)(2,1)}, f32[2,1024]{1,0:T(2,128)}) custom-call(bf16[128,14336]{1,0:T(8,128)(2,1)} %bitcast.10, bf16[128,4096]{1,0:T(8,128)(2,1)} %bitcast.11, bf16[64,3584]{1,0:T(8,128)(2,1)} %bitcast.12, bf16[64,1024]{1,0:T(8,128)(2,1)} %bitcast.13, bf16[256,2048]{1,0:T(8,128)(2,1)} %queries.1, ...), custom_call_target="tpu_custom_call" | custom-call | tf_op jit(solution)/shard_map/pallas_call | solution.py:291
  43.2 0.0 copy-start
  43.3 3.5 %convolution_multiply_fusion = f32[1024,1024]{1,0:T(8,128)} fusion(bf16[16,1024]{1,0:T(8,128)(2,1)} %get-tuple-element.5, bf16[16,1024]{1,0:T(8,128)(2,1)} %get-tuple-element.6), kind=kOutput, calls=%fused_computation | convolution fusion | flops 34603008 | bytes 4259840 | tf_op jit(solution)/shard_map/dot_general | solution.py:329
  46.8 0.0 copy-done
  46.8 0.6 %copy.9 = f32[2,1024]{1,0:T(2,128)} copy(f32[2,1024]{1,0:T(2,128)S(1)} %copy-done) | data formatting | bytes 16384
Async XLA Ops:
  43.2 3.5 %copy-start = (f32[2,1024]{1,0:T(2,128)S(1)}, f32[2,1024]{1,0:T(2,128)}, u32[]{:S(2)}) copy-start(f32[2,1024]{1,0:T(2,128)} %get-tuple-element.11) | copy-start | bytes 24580

commit v2 on v1

--- a/solution.py
+++ b/solution.py
@@ -10,18 +10,22 @@
 
 MESH = pl.DeviceIdType.MESH
 NT = (((1,), (1,)), ((), ()))
+PARTS = 3
+THIRD = PARTS // 3
+ITEMS = PARTS + THIRD
+LAG = 3
 
 
 def kernel(F, hidden, out_grad, pin, pout, queries, lengths,
            rows_out, cols_out, scores_out,
            buf, hid, ogr, qry, acc, part, summed, gath, flat, enc, spart, sgot,
-           local_sem, zs, xs, ys, dxs, dys, zr, xr, yr, dxr, dyr,
+           local_sem, zs, xs, ys, zr, xr, yr,
            sub_sem, es, er, ss, sr):
     g, f, d, s = (lax.axis_index(n) for n in ("groups", "fsdp", "dp", "sub"))
     W = pin.shape[0]
     kin, kout = pin.shape[1], pout.shape[1]
     L = kin + kout
-    half = L // 2
+    lanes = L // PARTS
     piece_rows = W // 4
     tokens = hidden.shape[0]
     E = enc.shape[0]
@@ -39,64 +43,55 @@
         for k in range(F)
     ]
     query_load = pltpu.make_async_copy(queries, qry, local_sem.at[2])
-    for load in loads:
+    for load in loads[:2]:
         load.start()
-    query_load.start()
 
     barrier = pltpu.get_barrier_semaphore()
-    others = [(df, dd, ds) for df in range(F) for dd in range(2) for ds in range(2)][1:]
-    for df, dd, ds in others:
-        pl.semaphore_signal(
-            barrier, inc=1,
-            device_id=(g, lax.rem(f + df, F), lax.rem(d + dd, 2), lax.rem(s + ds, 2)),
-            device_id_type=MESH,
-        )
-    pl.semaphore_signal(barrier, inc=1, device_id=(1 - g, f, d, s), device_id_type=MESH)
-    pl.semaphore_wait(barrier, len(others) + 1)
+    for dev in ((g, f, d, 1 - s), (g, f, 1 - d, s), (1 - g, f, d, s)):
+        pl.semaphore_signal(barrier, inc=1, device_id=dev, device_id_type=MESH)
+
+    @pl.when(f > 0)
+    def _():
+        pl.semaphore_signal(barrier, inc=1, device_id=(g, f - 1, d, s), device_id_type=MESH)
+
+    @pl.when(f < F - 1)
+    def _():
+        pl.semaphore_signal(barrier, inc=1, device_id=(g, f + 1, d, s), device_id_type=MESH)
+
+    pl.semaphore_wait(barrier, 3 + jnp.where(f > 0, 1, 0) + jnp.where(f < F - 1, 1, 0))
 
     mine = g * 2 + d
     col_x, col_y, col_d = g * 2 + (1 - d), (1 - g) * 2 + d, (1 - g) * 2 + (1 - d)
     dev_x, dev_y = (g, f, 1 - d, s), (1 - g, f, d, s)
 
-    def piece(shard, col, lanes=None):
+    def copy(shard, col, part, send, recv, dev):
         rows = pl.ds(pl.multiple_of(col * piece_rows, piece_rows), piece_rows)
-        if lanes is None:
-            return buf.at[shard, rows, :]
-        return buf.at[shard, rows, pl.ds(lanes * half, half)]
-
-    def copy(ref, send, recv, dev):
+        ref = buf.at[shard, rows, pl.ds(part * lanes, lanes)]
         return pltpu.make_async_remote_copy(
             src_ref=ref, dst_ref=ref, send_sem=send, recv_sem=recv,
             device_id=dev, device_id_type=MESH,
         )
 
-    def along_z(shard, up):
+    def along_z(shard, k, up):
         dev = (g, f + 1, d, s) if up else (g, f - 1, d, s)
-        return copy(piece(shard, mine), zs.at[1 if up else 0, shard], zr.at[shard], dev)
-
-    def to_x(shard):
-        return copy(piece(shard, mine), xs.at[shard], xr.at[shard], dev_x)
-
-    def to_y(shard):
-        return copy(piece(shard, mine), ys.at[shard], yr.at[shard], dev_y)
-
-    def from_x(shard):
-        return copy(piece(shard, col_x), xs.at[shard], xr.at[shard], dev_x)
-
-    def from_y(shard):
-        return copy(piece(shard, col_y), ys.at[shard], yr.at[shard], dev_y)
-
-    def x_on_to_y(shard):
-        return copy(piece(shard, col_x, 0), dys.at[shard], dyr.at[shard], dev_y)
-
-    def y_on_to_x(shard):
-        return copy(piece(shard, col_y, 1), dxs.at[shard], dxr.at[shard], dev_x)
-
-    def diag_by_y(shard):
-        return copy(piece(shard, col_d, 0), dys.at[shard], dyr.at[shard], dev_y)
-
-    def diag_by_x(shard):
-        return copy(piece(shard, col_d, 1), dxs.at[shard], dxr.at[shard], dev_x)
+        col, part = (mine, k) if k < PARTS else (col_d, k - THIRD)
+        return copy(shard, col, part, zs.at[1 if up else 0, shard, k], zr.at[shard, k], dev)
+
+    def to_x(shard, k):
+        col, part = (mine, k) if k < PARTS else (col_y, k - 2 * THIRD)
+        return copy(shard, col, part, xs.at[shard, k], xr.at[shard, k], dev_x)
+
+    def to_y(shard, k):
+        col, part = (mine, k) if k < PARTS else (col_x, k - PARTS)
+        return copy(shard, col, part, ys.at[shard, k], yr.at[shard, k], dev_y)
+
+    def from_x(shard, k):
+        col, part = (col_x, k) if k < PARTS else (col_d, k - 2 * THIRD)
+        return copy(shard, col, part, xs.at[shard, k], xr.at[shard, k], dev_x)
+
+    def from_y(shard, k):
+        col, part = (col_y, k) if k < PARTS else (col_d, k - PARTS)
+        return copy(shard, col, part, ys.at[shard, k], yr.at[shard, k], dev_y)
 
     def project(shard):
         acc[W:, :] += lax.dot_general(
@@ -104,62 +99,71 @@
         acc[:W, :] += lax.dot_general(
             buf[shard, :, kin:], ogr[shard], NT, preferred_element_type=jnp.float32)
 
-    def each(t, fn):
+    def each(t, fn, k=None):
         @pl.when(f - t >= 0)
         def _():
-            fn(f - t, True)
+            fn(f - t, True, k)
 
         @pl.when(f + t < F)
         def _():
-            fn(f + t, False)
+            fn(f + t, False, k)
+
+    def onward(shard, up, k, act):
+        if up:
+            @pl.when(f < F - 1)
+            def _():
+                act(along_z(shard, k, True))
+        else:
+            @pl.when(f > 0)
+            def _():
+                act(along_z(shard, k, False))
 
     loads[0].wait()
     loads[1].wait()
-
-    @pl.when(f > 0)
-    def _():
-        along_z(f, False).start()
-
-    @pl.when(f < F - 1)
-    def _():
-        along_z(f, True).start()
-
+    for k in range(ITEMS):
+        for up in (False, True):
+            onward(f, up, k, lambda c: c.start())
+
+    for load in loads[2:]:
+        load.start()
+    query_load.start()
     for load in loads[2:]:
         load.wait()
     acc[...] = jnp.zeros_like(acc)
     project(f)
 
-    def arrive(shard, up):
-        along_z(shard, up).wait_recv()
-        if up:
-            @pl.when(f < F - 1)
-            def _():
-                along_z(shard, True).start()
+    def arrive(shard, up, k):
+        along_z(shard, k, up).wait_recv()
+        onward(shard, up, k, lambda c: c.start())
+        if k < PARTS:
+            to_x(shard, k).start()
+            to_y(shard, k).start()
+
+    def relay(shard, up, k):
+        if k < THIRD:
+            from_x(shard, k).wait_recv()
+            to_y(shard, PARTS + k).start()
         else:
-            @pl.when(f > 0)
-            def _():
-                along_z(shard, False).start()
-        to_x(shard).start()
-        to_y(shard).start()
-
-    def relay(shard, up):
-        from_x(shard).wait_recv()
-        x_on_to_y(shard).start()
-        from_y(shard).wait_recv()
-        y_on_to_x(shard).start()
-
-    def finish(shard, up):
-        diag_by_y(shard).wait_recv()
-        diag_by_x(shard).wait_recv()
+            from_y(shard, k).wait_recv()
+            to_x(shard, PARTS + k - THIRD).start()
+
+    def finish(shard, up, k):
+        for k in range(THIRD, ITEMS):
+            from_x(shard, k).wait_recv()
+        for k in [*range(THIRD), *range(2 * THIRD, ITEMS)]:
+            from_y(shard, k).wait_recv()
         project(shard)
 
-    for t in range(1, F + 2):
-        if t < F:
-            each(t, arrive)
-        if 1 <= t - 1 < F:
-            each(t - 1, relay)
-        if 1 <= t - 2 < F:
-            each(t - 2, finish)
+    items = [(t, k) for t in range(1, F) for k in range(ITEMS)]
+    for n in range(len(items) + LAG):
+        if n < len(items):
+            each(items[n][0], arrive, items[n][1])
+        if n >= LAG and items[n - LAG][1] < 2 * THIRD:
+            each(items[n - LAG][0], relay, items[n - LAG][1])
+        if n < len(items) and items[n][0] > 1 and items[n][1] == ITEMS - 1:
+            each(items[n][0] - 1, finish)
+    if F > 1:
+        each(F - 1, finish)
 
     p_copy = pltpu.make_async_remote_copy(
         src_ref=acc, dst_ref=part, send_sem=sub_sem.at[0], recv_sem=sub_sem.at[1],
@@ -249,27 +253,15 @@
         enc_copy(k, pair, (g, pf, pd, s)).wait_send()
     p_copy.wait_send()
 
-    @pl.when(f > 0)
-    def _():
-        along_z(f, False).wait_send()
-
-    @pl.when(f < F - 1)
-    def _():
-        along_z(f, True).wait_send()
-
-    def sent(shard, up):
-        if up:
-            @pl.when(f < F - 1)
-            def _():
-                along_z(shard, True).wait_send()
-        else:
-            @pl.when(f > 0)
-            def _():
-                along_z(shard, False).wait_send()
-        to_x(shard).wait_send()
-        to_y(shard).wait_send()
-        x_on_to_y(shard).wait_send()
-        y_on_to_x(shard).wait_send()
+    for k in range(ITEMS):
+        for up in (False, True):
+            onward(f, up, k, lambda c: c.wait_send())
+
+    def sent(shard, up, k):
+        for k in range(ITEMS):
+            onward(shard, up, k, lambda c: c.wait_send())
+            to_x(shard, k).wait_send()
+            to_y(shard, k).wait_send()
 
     for t in range(1, F):
         each(t, sent)
@@ -284,7 +276,7 @@
     nq, dims = queries.shape
     E = F * 2 * examples
     KK = W * W
-    any_spec = pl.BlockSpec(memory_space=pl.ANY)
+    hbm = pl.BlockSpec(memory_space=pltpu.HBM)
     vmem = pl.BlockSpec(memory_space=pltpu.VMEM)
     bf, f32 = jnp.bfloat16, jnp.float32
     dma = pltpu.SemaphoreType.DMA
@@ -295,7 +287,7 @@
             jax.ShapeDtypeStruct((E, KK // 4), bf),
             jax.ShapeDtypeStruct((examples, nq * F), f32),
         ),
-        in_specs=[any_spec] * 5 + [pl.BlockSpec(memory_space=pltpu.SMEM)],
+        in_specs=[hbm] * 5 + [pl.BlockSpec(memory_space=pltpu.SMEM)],
         out_specs=(vmem, vmem, vmem),
         scratch_shapes=[
             pltpu.VMEM((F, W, kin + kout), bf),
@@ -311,8 +303,8 @@
             pltpu.VMEM((E // 2, 2, nq), f32),
             pltpu.VMEM((2 * F, 2, nq), f32),
             dma((3 + 2 * F,)),
-            dma((2, F)), dma((F,)), dma((F,)), dma((F,)), dma((F,)),
-            dma((F,)), dma((F,)), dma((F,)), dma((F,)), dma((F,)),
+            dma((2, F, ITEMS)), dma((F, ITEMS)), dma((F, ITEMS)),
+            dma((F, ITEMS)), dma((F, ITEMS)), dma((F, ITEMS)),
             dma((2,)),
             dma((2 * F,)), dma((2 * F,)), dma((2 * F,)), dma((2 * F,)),
         ],

time: 47.6 us -> 41.9 us (0.88)
  Pallas kernels: 42.6 us -> 36.9 us
    pallas_call x1, Pallas kernels: 42.6 us -> 36.9 us  [fused(): pl.pallas_call(functools.partial(kernel, F), out_shape=(jax.ShapeDtypeStr...]
where the time goes in v2:
time: 41.9 us; the launch traced here: 41.7 us
  Pallas kernels  36.9 us (88%)
  matrix products  3.53 us (8%)
  between operations  0.65 us (2%)
  local copies, waits for them, and re-layouts  0.6 us (1%)
    pallas_call x1, Pallas kernels, fused(): pl.pallas_call(functools.partial(kernel, F), out_shape=(jax.ShapeDtypeStr...  36.9 us
    dot_general x1, matrix products, fused(): lax.dot_general(rows, cols, (((0,), (0,)), ((), ())), preferred_element_t...  3.53 us

profile of v2, /device:TPU:0, one launch (start us, length us, event | category | flops | bytes accessed | tf_op | source)
XLA Modules:
  0.0 41.7 jit_solution(859129471943240167)
XLA Ops:
  0.6 36.9 %shard_map.77 = (bf16[16,1024]{1,0:T(8,128)(2,1)}, bf16[16,1024]{1,0:T(8,128)(2,1)}, f32[2,1024]{1,0:T(2,128)}) custom-call(bf16[128,14336]{1,0:T(8,128)(2,1)} %bitcast.10, bf16[128,4096]{1,0:T(8,128)(2,1)} %bitcast.11, bf16[64,3584]{1,0:T(8,128)(2,1)} %bitcast.12, bf16[64,1024]{1,0:T(8,128)(2,1)} %bitcast.13, bf16[256,2048]{1,0:T(8,128)(2,1)} %queries.1, ...), custom_call_target="tpu_custom_call" | custom-call | tf_op jit(solution)/shard_map/pallas_call | solution.py:283
  37.5 0.0 copy-start
  37.5 3.5 %convolution_multiply_fusion = f32[1024,1024]{1,0:T(8,128)} fusion(bf16[16,1024]{1,0:T(8,128)(2,1)} %get-tuple-element.5, bf16[16,1024]{1,0:T(8,128)(2,1)} %get-tuple-element.6), kind=kOutput, calls=%fused_computation | convolution fusion | flops 34603008 | bytes 4259840 | tf_op jit(solution)/shard_map/dot_general | solution.py:321
  41.1 0.0 copy-done
  41.1 0.6 %copy.9 = f32[2,1024]{1,0:T(2,128)} copy(f32[2,1024]{1,0:T(2,128)S(1)} %copy-done) | data formatting | bytes 16384
Async XLA Ops:
  37.5 3.5 %copy-start = (f32[2,1024]{1,0:T(2,128)S(1)}, f32[2,1024]{1,0:T(2,128)}, u32[]{:S(2)}) copy-start(f32[2,1024]{1,0:T(2,128)} %get-tuple-element.11) | copy-start | bytes 24580
